TPU v7x, 512 devices: a whole 4x4x16 slice. The times are simulated.
512 devices in a mesh: dp: 64 (over x, z), tensor: 8 (over y, core).
Axes of the slice: x: 4, y: 4, z: 16, core: 2. Of those that a mesh axis runs over, the one named last changes fastest.
Arguments:
- grad: bfloat16 [64, 768, 8192], P('dp', None, 'tensor'), may hold values from -6 to 6
- residual: bfloat16 [64, 768, 8192], P('dp', None, 'tensor'), may hold values from -4 to 4
- counts: int32 [64], P('dp'), may hold values from 1000 to 3499
- q_start: float32 [64, 8192], P(None, 'tensor'), may hold values from -0.0625 to 0.0625
Outputs:
- new_residual: bfloat16 [64, 768, 8192], P('dp', None, 'tensor')
- q_final: float32 [64, 8192], P(None, 'tensor')
All inputs are finite; a program needn't handle non-finite values.
Results may differ from a plain program's by a relative error of at most 0.001.
Values sent between devices are 32-bit elements; how exact they have to be, the bound alone decides.
A program may use at most 64 MiB of HBM per device.

v0:
```python
import jax
import jax.numpy as jnp
from jax import lax
from jax.sharding import PartitionSpec as P

ITERS = 2


def left_terms(q_basis, source):
    return jnp.einsum("kc,rc->kr", q_basis, source, precision=lax.Precision.HIGHEST)


def sum_left(partial_value):
    return lax.psum(partial_value, ("dp", "tensor"))


def local(grad, residual, counts, q_start):
    highest = lax.Precision.HIGHEST
    gradient = grad[0].astype(jnp.float32)
    carried = residual[0].astype(jnp.float32)
    tokens_here = counts.astype(jnp.float32)
    replicas = lax.axis_size("dp")
    q_basis = q_start
    token_total = lax.psum(tokens_here, "dp")[0]
    first_sum = jnp.zeros((q_basis.shape[0], gradient.shape[0]), jnp.float32)
    weight = replicas * tokens_here[0] / token_total
    matrix = weight * gradient + carried
    p_basis = first_sum
    for step_index in range(ITERS):
        p_sum = sum_left(left_terms(q_basis, matrix)) / replicas
        gram_matrix = jnp.dot(p_sum, p_sum.T, precision=highest)
        lower_factor = jnp.linalg.cholesky(gram_matrix)
        p_basis = jax.scipy.linalg.solve_triangular(lower_factor, p_sum, lower=True)
        right_part = jnp.einsum("kr,rc->kc", p_basis, matrix, precision=highest)
        q_basis = lax.psum(right_part, "dp") / replicas
    approx = jnp.einsum("kr,kc->rc", p_basis, q_basis, precision=highest)
    new_residual = (matrix - approx).astype(jnp.bfloat16)[None]
    return (new_residual, q_basis)


def solution(mesh):
    placed = (P("dp", None, "tensor"), P("dp", None, "tensor"), P("dp"), P(None, "tensor"))
    return jax.shard_map(
        local,
        mesh=mesh,
        in_specs=placed,
        out_specs=(P("dp", None, "tensor"), P(None, "tensor")),
        check_vma=False,
    )
```

profile of v0, /device:TPU:1, one launch (start us, length us, event | category | flops | bytes accessed | tf_op | source)
XLA Modules:
  0.0 1617.4 jit_solution(2289165099814927399)
XLA Ops:
  7.2 0.0 copy-start
  7.2 0.0 all-reduce.5.cloned.1.call-start
  7.9 123.1 %psum.35 = f32[1]{0:T(128)} all-reduce(f32[1]{0:T(128)S(6)} %convert_element_type.14), channel_id=1, replica_groups=mesh['dp'=64,'tensor'=8] {'dp'}, use_global_device_ids=true, to_apply=%region_0.0 | all-reduce | flops 1 | bytes 8 | tf_op jit(solution)/shard_map/psum | solution.py:24
  131.7 0.0 copy-done
  131.7 0.0 copy-start.1
  131.7 0.0 copy-start.2
  131.8 6.1 fusion.14
  137.9 0.0 all-reduce.5.cloned.1.call-update
  137.9 0.0 all-reduce.7.cloned.1.call-start
  138.0 471.3 %all-reduce.5.cloned.1.call-done = f32[64,768]{1,0:T(8,128)} async-done(((f32[64,768]{1,0:T(8,128)}), f32[64,768]{1,0:T(8,128)}) %all-reduce.5.cloned.1.call-update) | async-done | bytes 196624 | tf_op jit(solution)/shard_map/psum | solution.py:14
  609.3 1.3 fusion.24
  610.6 0.1 copy.6
  610.7 5.8 cholesky.44
  616.6 0.6 compare_reduce_fusion.1
  617.2 0.7 fusion.31
  617.9 4.9 custom-call.6
  622.8 1.3 fusion.22
  624.1 0.0 copy-done.1
  624.1 0.0 copy-done.2
  624.1 3.1 fusion.4
  627.2 0.0 all-reduce.7.cloned.1.call-update
  627.2 0.0 all-reduce.9.cloned.1.call-start
  627.3 247.0 %all-reduce.7.cloned.1.call-done = f32[64,1024]{1,0:T(8,128)} async-done(((f32[64,1024]{1,0:T(8,128)}), f32[64,1024]{1,0:T(8,128)}) %all-reduce.7.cloned.1.call-update) | async-done | bytes 262160 | tf_op jit(solution)/shard_map/psum | solution.py:35
  874.3 4.9 fusion.2
  879.1 0.0 all-reduce.9.cloned.1.call-update
  879.1 0.2 all-reduce.11.cloned.1.call-start
  879.4 459.8 %all-reduce.9.cloned.1.call-done = f32[64,768]{1,0:T(8,128)} async-done(((f32[64,768]{1,0:T(8,128)}), f32[64,768]{1,0:T(8,128)}) %all-reduce.9.cloned.1.call-update) | async-done | bytes 196624 | tf_op jit(solution)/shard_map/psum | solution.py:14
  1339.2 1.3 fusion.20
  1340.5 0.1 copy.7
  1340.6 5.8 cholesky.55
  1346.5 0.6 compare_reduce_fusion
  1347.1 0.7 fusion.32
  1347.8 4.9 custom-call.7
  1352.7 1.3 fusion.18
  1354.0 0.0 copy-start.3
  1354.0 0.7 copy-done.3
  1354.7 3.1 fusion
  1357.7 0.0 all-reduce.11.cloned.1.call-update
  1357.8 247.1 %all-reduce.11.cloned.1.call-done = f32[64,1024]{1,0:T(8,128)} async-done(((f32[64,1024]{1,0:T(8,128)}), f32[64,1024]{1,0:T(8,128)}) %all-reduce.11.cloned.1.call-update) | async-done | bytes 262160 | tf_op jit(solution)/shard_map/psum | solution.py:35
  1604.8 1.0 broadcast_multiply_fusion
  1605.8 0.0 copy-start.4
  1605.8 5.1 fusion.13
  1610.9 0.0 copy-done.4
  (4 shorter events, 0.1 us)
Async XLA Ops:
  7.2 124.6 %copy-start = (f32[64,1024]{1,0:T(8,128)S(1)}, f32[64,1024]{1,0:T(8,128)}, u32[]{:S(2)}) copy-start(f32[64,1024]{1,0:T(8,128)} %param.10) | copy-start | bytes 786436
  7.2 602.1 %all-reduce.5.cloned.1.call-start = ((), (), s32[]{:S(2)}) async-start(), calls=%async_computation | async-start | bytes 393216 | tf_op jit(solution)/shard_map/psum | solution.py:14
  131.7 492.4 %copy-start.1 = (bf16[1,768,1024]{2,1,0:T(8,128)(2,1)S(1)}, bf16[1,768,1024]{2,1,0:T(8,128)(2,1)}, u32[]{:S(2)}) copy-start(bf16[1,768,1024]{2,1,0:T(8,128)(2,1)} %param.8) | copy-start | bytes 4718596
  131.7 492.4 %copy-start.2 = (bf16[1,768,1024]{2,1,0:T(8,128)(2,1)S(1)}, bf16[1,768,1024]{2,1,0:T(8,128)(2,1)}, u32[]{:S(2)}) copy-start(bf16[1,768,1024]{2,1,0:T(8,128)(2,1)} %param.7) | copy-start | bytes 4718596
  137.9 736.4 %all-reduce.7.cloned.1.call-start = ((), (), s32[]{:S(2)}) async-start(), calls=%async_computation.1 | async-start | bytes 524288 | tf_op jit(solution)/shard_map/psum | solution.py:35
  627.2 711.9 %all-reduce.9.cloned.1.call-start = ((), (), s32[]{:S(2)}) async-start(), calls=%async_computation.2 | async-start | bytes 393216 | tf_op jit(solution)/shard_map/psum | solution.py:14
  879.1 725.7 %all-reduce.11.cloned.1.call-start = ((), (), s32[]{:S(2)}) async-start(), calls=%async_computation.3 | async-start | bytes 524288 | tf_op jit(solution)/shard_map/psum | solution.py:35
  1354.0 0.7 copy-start.3
  1605.8 5.1 copy-start.4
Sparse Core Ops, SparseCore 0:
  138.0 471.2 all-reduce.4
  627.3 246.8 all-reduce.6
  880.3 458.8 all-reduce.8
  1357.9 246.8 all-reduce.10
where the time goes:
time: 1630 us; the launch traced here: 1620 us
  waiting for transfers between devices  1430 us (88%)
  blocking collectives  123 us (8%)
  matrix products  27.5 us (2%)
  other arithmetic  25.1 us (2%)
    psum x2, waiting for transfers between devices, sum_left(): return lax.psum(partial_value, ('dp', 'tensor'))  931 us
    psum x2, waiting for transfers between devices, local(): q_basis = lax.psum(right_part, 'dp') / replicas  494 us
    psum x1, blocking collectives, local(): token_total = lax.psum(tokens_here, 'dp')[0]  123 us
  transfers between devices with their start and end apart: 4, of which 4 were waited for; matrix products, arithmetic and copies ran while one was open for 0% of the time, Pallas kernels for 0%

commit v1 on v0

v1 whole, which is shorter than its diff:
```python
import jax
import jax.numpy as jnp
from jax import lax
from jax.sharding import PartitionSpec as P
import jax.experimental.pallas as pl
import jax.experimental.pallas.tpu as pltpu

MESH = pl.DeviceIdType.MESH
HIGHEST = lax.Precision.HIGHEST
F32 = jnp.float32
BF16 = jnp.bfloat16
ROWS, RANK, WIDTH, REPLICAS = 768, 64, 1024, 64
HALF = ROWS // 2
NX, NY, NZ = 4, 4, 16
NN = (((1,), (0,)), ((), ()))
NT = (((1,), (1,)), ((), ()))
PARTNERS = 43


def split(value):
    high = value.astype(BF16)
    low = (value - high.astype(F32)).astype(BF16)
    return jnp.concatenate([high, low], axis=0)


def fold(value):
    return value[:RANK] + value[RANK:]


def place(x, z, y, c):
    return (x * NZ + z, y * 2 + c)


def near_z(o):
    return jnp.where(o == 3, NZ - 1, o)


def kernel(counts, q_start, grad, residual, new_residual, q_final,
           g, r, out, load_sem, store_sem,
           count_x, count_z, count_sem,
           part1, core1, rows1, zs1, part2, core2, rows2, zs2, pf, p_sem,
           qs, near, far, qf, q_sem, elim, p_left):
    dp = lax.axis_index("dp")
    tensor = lax.axis_index("tensor")
    x, z, y, c = dp // NZ, dp % NZ, tensor // 2, tensor % 2
    me = x * NY + y

    load_g = pltpu.make_async_copy(grad.at[0], g, load_sem.at[0])
    load_r = pltpu.make_async_copy(residual.at[0], r, load_sem.at[1])
    load_g.start()
    load_r.start()

    def core_peer():
        return place(x, z, y, 1 - c)

    def xy_peer(j):
        return (x + j % 4) % 4, (y + j // 4) % 4

    barrier = pltpu.get_barrier_semaphore()

    def announce(device):
        pl.semaphore_signal(barrier, inc=1, device_id=device, device_id_type=MESH)

    def announce_z(k, carry):
        announce(place(x, (z + k) % NZ, y, c))
        return carry

    def announce_xy(j, carry):
        px, py = xy_peer(j)
        announce(place(px, z, py, c))
        return carry

    def announce_xz(i, carry):
        o = i // 3
        dz = jnp.where(o < 2, o + 1, o + 12)
        announce(place((x + i % 3 + 1) % 4, (z + dz) % NZ, y, c))
        return carry

    lax.fori_loop(1, 16, announce_z, 0)
    lax.fori_loop(1, 16, announce_xy, 0)
    lax.fori_loop(0, 12, announce_xz, 0)
    announce(core_peer())

    def send(src, dst, sems, device):
        pltpu.make_async_remote_copy(
            src_ref=src, dst_ref=dst, send_sem=sems.at[0], recv_sem=sems.at[1],
            device_id=device, device_id_type=MESH,
        ).start()

    def took(ref, sem):
        pltpu.make_async_copy(ref, ref, sem).wait()

    def left_sum(step, part, core, rows, zs, finish, beside):
        sems = p_sem.at[step]
        send(part.at[1 - c], core, sems.at[0], core_peer())
        took(core, sems.at[0, 1])
        part[c] = part[c] + core[...]

        def to_xy(j, carry):
            px, py = xy_peer(j)
            send(part.at[c, px * NY + py], rows.at[j - 1], sems.at[1], place(px, z, py, c))
            return carry

        lax.fori_loop(1, 16, to_xy, 0)
        beside()
        took(rows, sems.at[1, 1])
        zs[z] = part[c, me] + jnp.sum(rows[...], axis=0)

        def to_z(k, carry):
            send(zs.at[z], zs.at[z], sems.at[2], place(x, (z + k) % NZ, y, c))
            return carry

        lax.fori_loop(1, 16, to_z, 0)
        took(zs.at[pl.ds(0, 15)], sems.at[2, 1])
        pf[step, c, me] = finish(jnp.sum(zs[...], axis=0))

        def spread(j, carry):
            px, py = xy_peer(j)
            send(pf.at[step, c, me], pf.at[step, c, me], sems.at[3], place(px, z, py, c))
            return carry

        lax.fori_loop(1, 16, spread, 0)
        took(pf.at[step, c, pl.ds(0, 15)], sems.at[3, 1])
        send(pf.at[step, c], pf.at[step, c], sems.at[4], core_peer())
        took(pf.at[step, 1 - c], sems.at[4, 1])
        took(core, sems.at[0, 0])
        took(rows, sems.at[1, 0])
        took(zs.at[pl.ds(0, 15)], sems.at[2, 0])
        took(pf.at[step, c, pl.ds(0, 15)], sems.at[3, 0])
        took(pf.at[step, c], sems.at[4, 0])
        halves = [
            jnp.concatenate([pf[step, h, s] for s in range(16)], axis=0) for h in range(2)
        ]
        return jnp.concatenate(halves, axis=1)

    def eliminate(first, last):
        lane = lax.broadcasted_iota(jnp.int32, (RANK, 2 * RANK), 1)
        sub = lax.broadcasted_iota(jnp.int32, (RANK, 1), 0)

        def one(j, carry):
            rows = elim[...]
            pivot = elim[pl.ds(j, 1), :]
            here = lane == (j + RANK)
            column = jnp.sum(jnp.where(here, rows, 0.0), axis=1, keepdims=True)
            diagonal = jnp.sum(jnp.where(here[:1], pivot, 0.0), axis=1, keepdims=True)
            factor = jnp.where(sub > j, column / diagonal, 0.0)
            elim[...] = rows - factor * pivot
            return carry

        lax.fori_loop(first, last, one, 0)

    def inverse():
        lane = lax.broadcasted_iota(jnp.int32, (RANK, 2 * RANK), 1)
        sub = lax.broadcasted_iota(jnp.int32, (RANK, 2 * RANK), 0)
        rows = elim[...]
        diagonal = jnp.sum(jnp.where(lane == sub + RANK, rows, 0.0), axis=1, keepdims=True)
        return rows[:, :RANK] / jnp.sqrt(diagonal)

    def right_sum(step, p_sum, weight):
        sems = q_sem.at[step]
        plain, weighted = split(p_sum), split(weight * p_sum)
        for jx in range(NX):
            cols = slice(256 * jx, 256 * (jx + 1))
            terms = fold(
                lax.dot_general(weighted, g[:, cols], NN, preferred_element_type=F32)
                + lax.dot_general(plain, r[:, cols], NN, preferred_element_type=F32)
            )
            for jz in range(4):
                qs[step, 4 * jx + jz] = terms[16 * jz:16 * (jz + 1)]
        slot = x * 4 + z % 4

        def to_near(i, carry):
            px, pz = (x + i % 4) % 4, (z + near_z(i // 4)) % NZ
            send(qs.at[step, px * 4 + pz % 4], near.at[step, i - 1], sems.at[0], place(px, pz, y, c))
            return carry

        lax.fori_loop(1, 16, to_near, 0)
        elim[...] = lax.dot_general(
            p_sum, jnp.concatenate([jnp.zeros_like(p_sum), p_sum], axis=0), NT,
            precision=HIGHEST, preferred_element_type=F32,
        ) + jnp.where(
            lax.broadcasted_iota(jnp.int32, (RANK, 2 * RANK), 0)
            == lax.broadcasted_iota(jnp.int32, (RANK, 2 * RANK), 1), 1.0, 0.0,
        )
        eliminate(0, 32)
        took(near.at[step], sems.at[0, 1])
        block = z // 4
        far[step, block] = qs[step, slot] + jnp.sum(near[step], axis=0)

        def to_far(k, carry):
            send(far.at[step, block], far.at[step, block], sems.at[1], place(x, (z + 4 * k) % NZ, y, c))
            return carry

        lax.fori_loop(1, 4, to_far, 0)
        eliminate(32, 64)
        lower_inverse = inverse()
        took(far.at[step, pl.ds(0, 3)], sems.at[1, 1])
        qf[step, slot] = jnp.sum(far[step], axis=0)

        def spread(i, carry):
            px, pz = (x + i % 4) % 4, (z + NZ - near_z(i // 4)) % NZ
            send(qf.at[step, slot], qf.at[step, slot], sems.at[2], place(px, pz, y, c))
            return carry

        lax.fori_loop(1, 16, spread, 0)
        p_basis = lax.dot_general(lower_inverse, p_sum, NN, precision=HIGHEST, preferred_element_type=F32)
        took(qf.at[step, pl.ds(0, 15)], sems.at[2, 1])
        took(near.at[step], sems.at[0, 0])
        took(far.at[step, pl.ds(0, 3)], sems.at[1, 0])
        took(qf.at[step, pl.ds(0, 15)], sems.at[2, 0])
        q_sum = jnp.concatenate(
            [jnp.concatenate([qf[step, 4 * jx + jz] for jz in range(4)], axis=0) for jx in range(NX)], axis=1
        )
        q_basis = lax.dot_general(
            lower_inverse, q_sum * (1.0 / REPLICAS), NN, precision=HIGHEST, preferred_element_type=F32
        )
        return p_basis, q_basis

    def put_part(ref, value, offset):
        for h in range(2):
            for s in range(16):
                ref[h, s, offset:offset + 4, :] = value[4 * s:4 * s + 4, HALF * h:HALF * (h + 1)]

    tokens = counts[0].astype(F32)
    first = split(q_start[...])
    load_g.wait()
    for n in range(3):
        rows = slice(256 * n, 256 * (n + 1))
        p_left[:, rows] = fold(lax.dot_general(first, g[rows], NT, preferred_element_type=F32)) * tokens
    put_part(part1, p_left[...], 0)
    load_r.wait()
    for n in range(3):
        rows = slice(256 * n, 256 * (n + 1))
        p_left[:, rows] = fold(lax.dot_general(first, r[rows], NT, preferred_element_type=F32))
    put_part(part1, p_left[...], 4)
    count_x[0] = jnp.full((8, 128), tokens, F32)
    pl.semaphore_wait(barrier, PARTNERS)

    def count_to_x(k, carry):
        send(count_x.at[0], count_x.at[k], count_sem.at[0], place((x + k) % 4, z, y, c))
        return carry

    lax.fori_loop(1, 4, count_to_x, 0)

    def count_over_z():
        took(count_x.at[pl.ds(1, 3)], count_sem.at[0, 1])
        count_z[z] = jnp.sum(count_x[...], axis=0)

        def count_to_z(k, carry):
            send(count_z.at[z], count_z.at[z], count_sem.at[1], place(x, (z + k) % NZ, y, c))
            return carry

        lax.fori_loop(1, 16, count_to_z, 0)

    def finish_first(total):
        took(count_z.at[pl.ds(0, 15)], count_sem.at[1, 1])
        all_tokens = jnp.sum(count_z[...], axis=0)[:1, :1]
        return (total[:4] * (REPLICAS / all_tokens) + total[4:]) * (1.0 / REPLICAS)

    p_sum = left_sum(0, part1, core1, rows1, zs1, finish_first, count_over_z)
    took(count_x.at[pl.ds(1, 3)], count_sem.at[0, 0])
    took(count_z.at[pl.ds(0, 15)], count_sem.at[1, 0])
    weight = REPLICAS * tokens / jnp.sum(count_z[...], axis=0)[:1, :1]
    p_basis, q_basis = right_sum(0, p_sum, weight)

    plain, weighted = split(q_basis), split(weight * q_basis)
    for n in range(3):
        rows = slice(256 * n, 256 * (n + 1))
        p_left[:, rows] = fold(
            lax.dot_general(weighted, g[rows], NT, preferred_element_type=F32)
            + lax.dot_general(plain, r[rows], NT, preferred_element_type=F32)
        )
    put_part(part2, p_left[...], 0)
    p_sum = left_sum(1, part2, core2, rows2, zs2, lambda total: total * (1.0 / REPLICAS), lambda: None)
    p_basis, q_basis = right_sum(1, p_sum, weight)

    q_final[...] = q_basis
    p_high = p_basis.astype(BF16).astype(F32)
    stacked = jnp.concatenate([p_high, p_basis - p_high, p_high], axis=0)
    left = stacked.T.astype(BF16)
    q_high = q_basis.astype(BF16)
    q_low = (q_basis - q_high.astype(F32)).astype(BF16)
    right = jnp.concatenate([q_high, q_high, q_low], axis=0)
    stores = []
    for n in range(6):
        rows = slice(128 * n, 128 * (n + 1))
        approx = lax.dot_general(left[rows], right, NN, preferred_element_type=F32)
        matrix = weight * g[rows].astype(F32) + r[rows].astype(F32)
        out[rows] = (matrix - approx).astype(BF16)
        store = pltpu.make_async_copy(out.at[rows], new_residual.at[0, rows], store_sem.at[n])
        store.start()
        stores.append(store)
    for store in stores:
        store.wait()


def local(grad, residual, counts, q_start):
    vmem = pl.BlockSpec(memory_space=pltpu.VMEM)
    anywhere = pl.BlockSpec(memory_space=pl.ANY)
    dma = pltpu.SemaphoreType.DMA
    return pl.pallas_call(
        kernel,
        out_shape=(
            jax.ShapeDtypeStruct((1, ROWS, WIDTH), BF16),
            jax.ShapeDtypeStruct((RANK, WIDTH), F32),
        ),
        in_specs=[pl.BlockSpec(memory_space=pltpu.SMEM), vmem, anywhere, anywhere],
        out_specs=(anywhere, vmem),
        scratch_shapes=[
            pltpu.VMEM((ROWS, WIDTH), BF16),
            pltpu.VMEM((ROWS, WIDTH), BF16),
            pltpu.VMEM((ROWS, WIDTH), BF16),
            dma((2,)),
            dma((6,)),
            pltpu.VMEM((4, 8, 128), F32),
            pltpu.VMEM((16, 8, 128), F32),
            dma((2, 2)),
            pltpu.VMEM((2, 16, 8, HALF), F32),
            pltpu.VMEM((16, 8, HALF), F32),
            pltpu.VMEM((15, 8, HALF), F32),
            pltpu.VMEM((16, 8, HALF), F32),
            pltpu.VMEM((2, 16, 4, HALF), F32),
            pltpu.VMEM((16, 4, HALF), F32),
            pltpu.VMEM((15, 4, HALF), F32),
            pltpu.VMEM((16, 4, HALF), F32),
            pltpu.VMEM((2, 2, 16, 4, HALF), F32),
            dma((2, 5, 2)),
            pltpu.VMEM((2, 16, 16, 256), F32),
            pltpu.VMEM((2, 15, 16, 256), F32),
            pltpu.VMEM((2, 4, 16, 256), F32),
            pltpu.VMEM((2, 16, 16, 256), F32),
            dma((2, 3, 2)),
            pltpu.VMEM((RANK, 2 * RANK), F32),
            pltpu.VMEM((RANK, ROWS), F32),
        ],
        compiler_params=pltpu.CompilerParams(
            collective_id=0, has_side_effects=True, vmem_limit_bytes=40 * 1024 * 1024
        ),
        name="power_step",
    )(counts, q_start, grad, residual)


def solution(mesh):
    placed = (P("dp", None, "tensor"), P("dp", None, "tensor"), P("dp"), P(None, "tensor"))
    return jax.shard_map(
        local,
        mesh=mesh,
        in_specs=placed,
        out_specs=(P("dp", None, "tensor"), P(None, "tensor")),
        check_vma=False,
    )
```

time: 1630 us -> 120 us (0.07)
  waiting for transfers between devices: 1430 us -> 0 us
  blocking collectives: 123 us -> 0 us
  Pallas kernels: 0 us -> 113 us
  matrix products: 27.5 us -> 0 us
  other arithmetic: 25.1 us -> 0 us
    psum x4 -> x0, waiting for transfers between devices: 1430 us -> none  [the longest x2 931 us: sum_left(): return lax.psum(partial_value, ('dp', 'tensor'))]
    psum x1 -> x0, blocking collectives: 123 us -> none  [local(): token_total = lax.psum(tokens_here, 'dp')[0]]
    pallas_call x0 -> x1, Pallas kernels: none -> 113 us  [local(): pl.pallas_call(kernel, out_shape=(jax.ShapeDtypeStruct((1, ROWS, WIDTH),...]
    dot_general x7 -> x0, matrix products: 24.9 us -> none  [the longest x2 11 us: left_terms(): jnp.einsum('kc,rc->kr', q_basis, source, precision=lax.Precision.HIGHEST)]
    another operation x10 -> x0, other arithmetic: 24.1 us -> none  [the longest x6 13 us: local(): lower_factor = jnp.linalg.cholesky(gram_matrix)]
  transfers between devices with their start and end apart: 4 -> 0, of which waited for: 4 -> 0; matrix products, arithmetic and copies ran while one was open for 0% -> 0% of each run, Pallas kernels for 0% -> 0%
where the time goes in v1:
time: 120 us
  Pallas kernels  113 us (94%)
  local copies, waits for them, and re-layouts  5.61 us (5%)
  between operations  1.3 us (1%)
    pallas_call x1, Pallas kernels, local(): pl.pallas_call(kernel, out_shape=(jax.ShapeDtypeStruct((1, ROWS, WIDTH),...  113 us
    unnamed x8, local copies, waits for them, and re-layouts  5.61 us

profile of v1, /device:TPU:1, one launch (start us, length us, event | category | flops | bytes accessed | tf_op | source)
XLA Modules:
  0.0 119.6 jit_solution(8860701109731666997)
XLA Ops:
  1.3 0.0 copy-start
  1.3 1.4 %copy-done = bf16[1,768,1024]{2,1,0:T(8,128)(2,1)S(1)} copy-done((bf16[1,768,1024]{2,1,0:T(8,128)(2,1)S(1)}, bf16[1,768,1024]{2,1,0:T(8,128)(2,1)}, u32[]{:S(2)}) %copy-start) | copy-done | bytes 1572888
  2.7 0.0 copy-start.1
  2.7 1.4 %copy-done.1 = bf16[1,768,1024]{2,1,0:T(8,128)(2,1)S(1)} copy-done((bf16[1,768,1024]{2,1,0:T(8,128)(2,1)S(1)}, bf16[1,768,1024]{2,1,0:T(8,128)(2,1)}, u32[]{:S(2)}) %copy-start.1) | copy-done | bytes 1572888
  4.1 0.0 copy-start.2
  4.1 0.9 copy-done.2
  5.0 112.7 %power_step.1 = (bf16[1,768,1024]{2,1,0:T(8,128)(2,1)S(1)}, f32[64,1024]{1,0:T(8,128)S(1)}) custom-call(s32[1]{0:T(128)S(6)} %copy.8.counts, f32[64,1024]{1,0:T(8,128)S(1)} %copy-done.2, bf16[1,768,1024]{2,1,0:T(8,128)(2,1)S(1)} %copy-done, bf16[1,768,1024]{2,1,0:T(8,128)(2,1)S(1)} %copy-done.1), custom_call_target="tpu_custom_call" | custom-call | tf_op jit(solution)/shard_map/power_step/pallas_call | solution.py:301
  117.8 1.1 copy.9
  118.9 0.7 copy.10
Async XLA Ops:
  1.3 1.4 %copy-start = (bf16[1,768,1024]{2,1,0:T(8,128)(2,1)S(1)}, bf16[1,768,1024]{2,1,0:T(8,128)(2,1)}, u32[]{:S(2)}) copy-start(bf16[1,768,1024]{2,1,0:T(8,128)(2,1)} %grad.1) | copy-start | bytes 4718596
  2.7 1.4 %copy-start.1 = (bf16[1,768,1024]{2,1,0:T(8,128)(2,1)S(1)}, bf16[1,768,1024]{2,1,0:T(8,128)(2,1)}, u32[]{:S(2)}) copy-start(bf16[1,768,1024]{2,1,0:T(8,128)(2,1)} %residual.1) | copy-start | bytes 4718596
  4.1 0.9 copy-start.2

commit v2 on v0

v2 whole, which is shorter than its diff:
```python
import jax
import jax.numpy as jnp
from jax import lax
from jax.sharding import PartitionSpec as P
import jax.experimental.pallas as pl
import jax.experimental.pallas.tpu as pltpu

MESH = pl.DeviceIdType.MESH
HIGHEST = lax.Precision.HIGHEST
F32 = jnp.float32
BF16 = jnp.bfloat16
ROWS, RANK, WIDTH, REPLICAS = 768, 64, 1024, 64
HALF, BAND = ROWS // 2, WIDTH // 4
NX, NY, NZ = 4, 4, 16
NN = (((1,), (0,)), ((), ()))
NT = (((1,), (1,)), ((), ()))
PARTNERS = 43
RING4 = (2, 1, 3, 0)
RING16 = (8, 7, 9, 6, 10, 5, 11, 4, 12, 3, 13, 2, 14, 1, 15)
PLANE = tuple((i, j) for i in RING4 for j in RING4 if (i, j) != (0, 0))
WINDOW = {0: 0, 1: 1, 2: 2, 3: -1}


def split(value):
    high = value.astype(BF16)
    return high, (value - high.astype(F32)).astype(BF16)


def tall(value):
    return jnp.concatenate(split(value), axis=0)


def fold(value):
    return value[:RANK] + value[RANK:]


def left_factor(value):
    high, low = split(value)
    return jnp.concatenate([high, high, low, low], axis=1)


def right_factor(value):
    high, low = split(value)
    return jnp.concatenate([high, low, high, low], axis=0)


def dot(a, b, dims):
    return lax.dot_general(a, b, dims, preferred_element_type=F32)


def place(x, z, y, c):
    return (x * NZ + z, y * 2 + c)


def kernel(counts, q_start, grad, residual, new_residual, q_final,
           q0, g, r, out, load_sem, store_sem,
           count_x, count_z, count_sem,
           part1, core1, rows1, zs1, part2, core2, rows2, zs2, pf, p_sem,
           qs, near, far, qf, q_sem, spread_sem, elim, p_acc):
    dp = lax.axis_index("dp")
    tensor = lax.axis_index("tensor")
    x, z, y, c = dp // NZ, dp % NZ, tensor // 2, tensor % 2
    me = x * NY + y
    turn = 1 - 2 * c

    load_q = pltpu.make_async_copy(q_start, q0, load_sem.at[0])
    load_g = pltpu.make_async_copy(grad.at[0], g, load_sem.at[1])
    load_r = pltpu.make_async_copy(residual.at[0], r, load_sem.at[2])
    load_q.start()
    load_g.start()
    load_r.start()

    def at_z(k):
        return place(x, (z + k) % NZ, y, c)

    def window_z(o):
        return (z + turn * WINDOW[o] + NZ) % NZ

    def window_back(o):
        return (z - turn * WINDOW[o] + NZ) % NZ

    core_peer = place(x, z, y, 1 - c)
    barrier = pltpu.get_barrier_semaphore()

    def announce(device):
        pl.semaphore_signal(barrier, inc=1, device_id=device, device_id_type=MESH)

    for k in RING16:
        announce(at_z(k))
    for dx, dy in PLANE:
        announce(place((x + dx) % NX, z, (y + dy) % NY, c))
    for dx in (2, 1, 3):
        for dz in (2, 14, 1, 15):
            announce(place((x + dx) % NX, (z + dz) % NZ, y, c))
    announce(core_peer)

    def send(src, dst, sems, device):
        pltpu.make_async_remote_copy(
            src_ref=src, dst_ref=dst, send_sem=sems[0], recv_sem=sems[1],
            device_id=device, device_id_type=MESH,
        ).start()

    def took(ref, sem):
        pltpu.make_async_copy(ref, ref, sem).wait()

    sent = []

    def pair(sems, i):
        return sems.at[i, 0], sems.at[i, 1]

    def half_rows(h):
        return pl.ds(pl.multiple_of(h * HALF, HALF), HALF)

    def band_cols(jx):
        return pl.ds(pl.multiple_of(jx * BAND, BAND), BAND)

    def put_part(ref, h, value, offset):
        for s in range(16):
            ref[h, s, offset:offset + 4, :] = value[4 * s:4 * s + 4]

    def left_sum(step, part, core, rows, zs, own_half, finish, after_core, after_xy):
        sems = p_sem.at[step]
        send(part.at[1 - c], core, pair(sems, 0), core_peer)
        sent.append((core, sems.at[0, 0]))
        after_core()
        own_half()
        took(core, sems.at[0, 1])
        for dx, dy in PLANE:
            px, py = (x + dx) % NX, (y + dy) % NY
            slot = px * NY + py
            part[c, slot] = part[c, slot] + core[slot]
            send(part.at[c, slot], rows.at[dx * NY + dy - 1], pair(sems, 1), place(px, z, py, c))
        sent.append((rows, sems.at[1, 0]))
        after_xy()
        part[c, me] = part[c, me] + core[me]
        took(rows, sems.at[1, 1])
        zs[z] = part[c, me] + jnp.sum(rows[...], axis=0)
        for k in RING16:
            send(zs.at[z], zs.at[z], pair(sems, 2), at_z(k))
        sent.append((zs.at[pl.ds(0, 15)], sems.at[2, 0]))
        took(zs.at[pl.ds(0, 15)], sems.at[2, 1])
        pf[step, c, me] = finish(jnp.sum(zs[...], axis=0))
        for dx, dy in PLANE:
            device = place((x + dx) % NX, z, (y + dy) % NY, c)
            send(pf.at[step, c, me], pf.at[step, c, me], pair(sems, 3), device)
        sent.append((pf.at[step, c, pl.ds(0, 15)], sems.at[3, 0]))
        took(pf.at[step, c, pl.ds(0, 15)], sems.at[3, 1])
        send(pf.at[step, c], pf.at[step, c], pair(sems, 4), core_peer)
        sent.append((pf.at[step, c], sems.at[4, 0]))

    def half_of(step, h):
        return jnp.concatenate([pf[step, h, s] for s in range(16)], axis=0)

    def eliminate(first, last):
        lane = lax.broadcasted_iota(jnp.int32, (RANK, 2 * RANK), 1)
        sub = lax.broadcasted_iota(jnp.int32, (RANK, 1), 0)

        def one(j, carry):
            rows = elim[...]
            pivot = elim[pl.ds(j, 1), :]
            here = lane == (j + RANK)
            column = jnp.sum(jnp.where(here, rows, 0.0), axis=1, keepdims=True)
            diagonal = jnp.sum(jnp.where(here[:1], pivot, 0.0), axis=1, keepdims=True)
            factor = jnp.where(sub > j, column / diagonal, 0.0)
            elim[...] = rows - factor * pivot
            return carry

        lax.fori_loop(first, last, one, 0)

    def inverse():
        lane = lax.broadcasted_iota(jnp.int32, (RANK, 2 * RANK), 1)
        sub = lax.broadcasted_iota(jnp.int32, (RANK, 2 * RANK), 0)
        rows = elim[...]
        diagonal = jnp.sum(jnp.where(lane == sub + RANK, rows, 0.0), axis=1, keepdims=True)
        return rows[:, :RANK] / jnp.sqrt(diagonal)

    def right_sum(step, weight, use):
        sems = q_sem.at[step]
        own = half_of(step, c)
        plain, weighted = tall(own), tall(weight * own)
        for jx in range(NX):
            cols = slice(BAND * jx, BAND * (jx + 1))
            terms = dot(weighted, g[half_rows(c), cols], NN) + dot(plain, r[half_rows(c), cols], NN)
            qs[step, jx] = fold(terms).reshape(4, 16, BAND)
        took(pf.at[step, 1 - c], p_sem.at[step, 4, 1])
        other = half_of(step, 1 - c)
        plain, weighted = tall(other), tall(weight * other)
        for dx in RING4:
            px = (x + dx) % NX
            rows, cols = half_rows(1 - c), band_cols(px)
            terms = dot(weighted, g[rows, cols], NN) + dot(plain, r[rows, cols], NN)
            qs[step, px] = qs[step, px] + fold(terms).reshape(4, 16, BAND)
            for o in RING4:
                if (dx, o) != (0, 0):
                    pz = window_z(o)
                    send(qs.at[step, px, pz % 4], near.at[step, dx * 4 + o - 1], pair(sems, 0), place(px, pz, y, c))
        sent.append((near.at[step], sems.at[0, 0]))
        p_sum = jnp.concatenate([half_of(step, 0), half_of(step, 1)], axis=1)
        diagonal = (
            lax.broadcasted_iota(jnp.int32, (RANK, 2 * RANK), 0)
            == lax.broadcasted_iota(jnp.int32, (RANK, 2 * RANK), 1)
        )
        elim[...] = lax.dot_general(
            p_sum, jnp.concatenate([jnp.zeros_like(p_sum), p_sum], axis=0), NT,
            precision=HIGHEST, preferred_element_type=F32,
        ) + jnp.where(diagonal, 1.0, 0.0)
        eliminate(0, 28)
        took(near.at[step], sems.at[0, 1])
        block = z // 4
        far[step, block] = qs[step, x, z % 4] + jnp.sum(near[step], axis=0)
        for k in (8, 4, 12):
            send(far.at[step, block], far.at[step, block], pair(sems, 1), at_z(k))
        sent.append((far.at[step, pl.ds(0, 3)], sems.at[1, 0]))
        eliminate(28, 64)
        took(far.at[step, pl.ds(0, 3)], sems.at[1, 1])
        qf[step, x, z % 4] = jnp.sum(far[step], axis=0)
        mine = qf.at[step, x, z % 4]
        for dx in RING4:
            for o in RING4:
                if (dx, o) != (0, 0):
                    send(mine, mine, (sems.at[2, 0], spread_sem.at[step, x]), place((x + dx) % NX, window_back(o), y, c))
        for n in range(3):
            sent.append((qf.at[step, n], sems.at[2, 0]))
        sent.append((qf.at[step, 0, pl.ds(0, 3)], sems.at[2, 0]))
        use(inverse(), p_sum)

    def bands(step, inverse_left):
        for dx in (0, 1, 3, 2):
            px = (x + dx) % NX
            if dx == 0:
                took(qf.at[step, x, pl.ds(0, 3)], spread_sem.at[step, x])
            else:
                took(qf.at[step, px], spread_sem.at[step, px])
            band = qf[step, px].reshape(RANK, BAND) * (1.0 / REPLICAS)
            yield dx, band_cols(px), dot(inverse_left, right_factor(band), NN)

    tokens = counts[0].astype(F32)
    load_q.wait()
    first = tall(q0[...])
    load_g.wait()
    load_r.wait()
    for h in (0, 1):
        rows = slice(HALF * h, HALF * (h + 1))
        put_part(part1, h, fold(dot(first, g[rows], NT)) * tokens, 0)
        put_part(part1, h, fold(dot(first, r[rows], NT)), 4)
    count_x[0] = jnp.full((1, 128), tokens, F32)
    pl.semaphore_wait(barrier, PARTNERS)

    def count_to_x():
        for k in (2, 1, 3):
            send(count_x.at[0], count_x.at[k], pair(count_sem, 0), place((x + k) % NX, z, y, c))
        sent.append((count_x.at[pl.ds(1, 3)], count_sem.at[0, 0]))

    def count_to_z():
        took(count_x.at[pl.ds(1, 3)], count_sem.at[0, 1])
        count_z[z] = jnp.sum(count_x[...], axis=0)
        for k in RING16:
            send(count_z.at[z], count_z.at[z], pair(count_sem, 1), at_z(k))
        sent.append((count_z.at[pl.ds(0, 15)], count_sem.at[1, 0]))

    def finish_first(total):
        took(count_z.at[pl.ds(0, 15)], count_sem.at[1, 1])
        all_tokens = jnp.sum(count_z[...], axis=0)[:, :1]
        return (total[:4] * (REPLICAS / all_tokens) + total[4:]) * (1.0 / REPLICAS)

    nothing = lambda: None
    left_sum(0, part1, core1, rows1, zs1, nothing, finish_first, count_to_x, count_to_z)
    weight = REPLICAS * tokens / jnp.sum(count_z[...], axis=0)[:, :1]

    kept = []
    right_sum(0, weight, lambda lower_inverse, p_sum: kept.append(left_factor(lower_inverse)))
    inverse_left = kept.pop()

    def left_terms(plain, weighted, h, cols):
        rows = half_rows(h)
        return fold(dot(weighted, g[rows, cols], NT) + dot(plain, r[rows, cols], NT))

    for dx, cols, band in bands(0, inverse_left):
        plain, weighted = tall(band), tall(weight * band)
        terms = left_terms(plain, weighted, 1 - c, cols)
        if dx == 0:
            p_acc[1 - c] = terms
        elif dx != 2:
            p_acc[1 - c] = p_acc[1 - c] + terms
        else:
            put_part(part2, 1 - c, p_acc[1 - c] + terms, 0)
            break
        terms = left_terms(plain, weighted, c, cols)
        p_acc[c] = terms if dx == 0 else p_acc[c] + terms

    def own_half():
        put_part(part2, c, p_acc[c] + left_terms(plain, weighted, c, cols), 0)

    left_sum(1, part2, core2, rows2, zs2, own_half, lambda total: total * (1.0 / REPLICAS), nothing, nothing)

    def last_left(lower_inverse, p_sum):
        p_basis = lax.dot_general(lower_inverse, p_sum, NN, precision=HIGHEST, preferred_element_type=F32)
        high = p_basis.astype(BF16).astype(F32)
        low = p_basis - high
        kept.append(left_factor(lower_inverse))
        kept.append(jnp.concatenate([high, high, low, low], axis=0).T.astype(BF16))

    right_sum(1, weight, last_left)
    p_left = kept.pop()
    inverse_left = kept.pop()
    stores = []
    for dx, cols, band in bands(1, inverse_left):
        q_final[:, cols] = band
        approx = dot(p_left, right_factor(band), NN)
        matrix = weight * g[:, cols].astype(F32) + r[:, cols].astype(F32)
        out[:, cols] = (matrix - approx).astype(BF16)
        store = pltpu.make_async_copy(out.at[:, cols], new_residual.at[0, :, cols], store_sem.at[dx])
        store.start()
        stores.append(store)
    for store in stores:
        store.wait()
    for ref, sem in sent:
        took(ref, sem)


def local(grad, residual, counts, q_start):
    vmem = pl.BlockSpec(memory_space=pltpu.VMEM)
    anywhere = pl.BlockSpec(memory_space=pl.ANY)
    dma = pltpu.SemaphoreType.DMA
    return pl.pallas_call(
        kernel,
        out_shape=(
            jax.ShapeDtypeStruct((1, ROWS, WIDTH), BF16),
            jax.ShapeDtypeStruct((RANK, WIDTH), F32),
        ),
        in_specs=[pl.BlockSpec(memory_space=pltpu.SMEM), anywhere, anywhere, anywhere],
        out_specs=(anywhere, vmem),
        scratch_shapes=[
            pltpu.VMEM((RANK, WIDTH), F32),
            pltpu.VMEM((ROWS, WIDTH), BF16),
            pltpu.VMEM((ROWS, WIDTH), BF16),
            pltpu.VMEM((ROWS, WIDTH), BF16),
            dma((3,)),
            dma((4,)),
            pltpu.VMEM((4, 1, 128), F32),
            pltpu.VMEM((16, 1, 128), F32),
            dma((2, 2)),
            pltpu.VMEM((2, 16, 8, HALF), F32),
            pltpu.VMEM((16, 8, HALF), F32),
            pltpu.VMEM((15, 8, HALF), F32),
            pltpu.VMEM((16, 8, HALF), F32),
            pltpu.VMEM((2, 16, 4, HALF), F32),
            pltpu.VMEM((16, 4, HALF), F32),
            pltpu.VMEM((15, 4, HALF), F32),
            pltpu.VMEM((16, 4, HALF), F32),
            pltpu.VMEM((2, 2, 16, 4, HALF), F32),
            dma((2, 5, 2)),
            pltpu.VMEM((2, 4, 4, 16, BAND), F32),
            pltpu.VMEM((2, 15, 16, BAND), F32),
            pltpu.VMEM((2, 4, 16, BAND), F32),
            pltpu.VMEM((2, 4, 4, 16, BAND), F32),
            dma((2, 3, 2)),
            dma((2, 4)),
            pltpu.VMEM((RANK, 2 * RANK), F32),
            pltpu.VMEM((2, RANK, HALF), F32),
        ],
        compiler_params=pltpu.CompilerParams(
            collective_id=0, has_side_effects=True, vmem_limit_bytes=60 * 1024 * 1024
        ),
        name="power_step",
    )(counts, q_start, grad, residual)


def solution(mesh):
    placed = (P("dp", None, "tensor"), P("dp", None, "tensor"), P("dp"), P(None, "tensor"))
    return jax.shard_map(
        local,
        mesh=mesh,
        in_specs=placed,
        out_specs=(P("dp", None, "tensor"), P(None, "tensor")),
        check_vma=False,
    )
```

time: 1630 us -> 107 us (0.07)
  waiting for transfers between devices: 1430 us -> 0 us
  blocking collectives: 123 us -> 0 us
  Pallas kernels: 0 us -> 102 us
  matrix products: 27.5 us -> 0 us
  other arithmetic: 25.1 us -> 0 us
    psum x4 -> x0, waiting for transfers between devices: 1430 us -> none  [the longest x2 931 us: sum_left(): return lax.psum(partial_value, ('dp', 'tensor'))]
    psum x1 -> x0, blocking collectives: 123 us -> none  [local(): token_total = lax.psum(tokens_here, 'dp')[0]]
    pallas_call x0 -> x1, Pallas kernels: none -> 102 us  [local(): pl.pallas_call(kernel, out_shape=(jax.ShapeDtypeStruct((1, ROWS, WIDTH),...]
    dot_general x7 -> x0, matrix products: 24.9 us -> none  [the longest x2 11 us: left_terms(): jnp.einsum('kc,rc->kr', q_basis, source, precision=lax.Precision.HIGHEST)]
    another operation x10 -> x0, other arithmetic: 24.1 us -> none  [the longest x6 13 us: local(): lower_factor = jnp.linalg.cholesky(gram_matrix)]
  transfers between devices with their start and end apart: 4 -> 0, of which waited for: 4 -> 0; matrix products, arithmetic and copies ran while one was open for 0% -> 0% of each run, Pallas kernels for 0% -> 0%
where the time goes in v2:
time: 107 us
  Pallas kernels  102 us (95%)
  local copies, waits for them, and re-layouts  3.42 us (3%)
  between operations  1.29 us (1%)
    pallas_call x1, Pallas kernels, local(): pl.pallas_call(kernel, out_shape=(jax.ShapeDtypeStruct((1, ROWS, WIDTH),...  102 us
    unnamed x4, local copies, waits for them, and re-layouts  3.42 us

profile of v2, /device:TPU:1, one launch (start us, length us, event | category | flops | bytes accessed | tf_op | source)
XLA Modules:
  0.0 106.7 jit_solution(1472625381636279976)
XLA Ops:
  1.3 102.0 %power_step.1 = (bf16[1,768,1024]{2,1,0:T(8,128)(2,1)}, f32[64,1024]{1,0:T(8,128)}) custom-call(s32[1]{0:T(128)S(6)} %copy.8.counts, f32[64,1024]{1,0:T(8,128)} %q_start.1, bf16[1,768,1024]{2,1,0:T(8,128)(2,1)} %grad.1, bf16[1,768,1024]{2,1,0:T(8,128)(2,1)} %residual.1), custom_call_target="tpu_custom_call" | custom-call | tf_op jit(solution)/shard_map/power_step/pallas_call | solution.py:325
  103.3 0.0 copy-start
  103.3 2.7 %copy.9 = bf16[1,768,1024]{2,1,0:T(8,128)(2,1)} copy(bf16[1,768,1024]{2,1,0:T(8,128)(2,1)} %get-tuple-element.4) | data formatting | bytes 3145728
  106.0 0.0 copy-done
  106.0 0.7 copy.10
Async XLA Ops:
  103.3 2.7 %copy-start = (f32[64,1024]{1,0:T(8,128)S(1)}, f32[64,1024]{1,0:T(8,128)}, u32[]{:S(2)}) copy-start(f32[64,1024]{1,0:T(8,128)} %get-tuple-element.5) | copy-start | bytes 786436

commit v3 on v2

--- a/solution.py
+++ b/solution.py
@@ -14,10 +14,10 @@
 NX, NY, NZ = 4, 4, 16
 NN = (((1,), (0,)), ((), ()))
 NT = (((1,), (1,)), ((), ()))
-PARTNERS = 43
+PARTNERS = 58
 RING4 = (2, 1, 3, 0)
 RING16 = (8, 7, 9, 6, 10, 5, 11, 4, 12, 3, 13, 2, 14, 1, 15)
-PLANE = tuple((i, j) for i in RING4 for j in RING4 if (i, j) != (0, 0))
+PLANE = tuple((i, j) for i in RING4 for j in RING4)
 WINDOW = {0: 0, 1: 1, 2: 2, 3: -1}
 
 
@@ -53,9 +53,9 @@
 
 
 def kernel(counts, q_start, grad, residual, new_residual, q_final,
-           q0, g, r, out, load_sem, store_sem,
+           q0, g, r, load_sem,
            count_x, count_z, count_sem,
-           part1, core1, rows1, zs1, part2, core2, rows2, zs2, pf, p_sem,
+           part1, rows1, zs1, part2, rows2, zs2, pf, p_sem,
            qs, near, far, qf, q_sem, spread_sem, elim, p_acc):
     dp = lax.axis_index("dp")
     tensor = lax.axis_index("tensor")
@@ -79,7 +79,6 @@
     def window_back(o):
         return (z - turn * WINDOW[o] + NZ) % NZ
 
-    core_peer = place(x, z, y, 1 - c)
     barrier = pltpu.get_barrier_semaphore()
 
     def announce(device):
@@ -88,11 +87,12 @@
     for k in RING16:
         announce(at_z(k))
     for dx, dy in PLANE:
-        announce(place((x + dx) % NX, z, (y + dy) % NY, c))
+        for core in (1, 0):
+            if (dx, dy, core) != (0, 0, 0):
+                announce(place((x + dx) % NX, z, (y + dy) % NY, (c + core) % 2))
     for dx in (2, 1, 3):
         for dz in (2, 14, 1, 15):
             announce(place((x + dx) % NX, (z + dz) % NZ, y, c))
-    announce(core_peer)
 
     def send(src, dst, sems, device):
         pltpu.make_async_remote_copy(
@@ -118,35 +118,35 @@
         for s in range(16):
             ref[h, s, offset:offset + 4, :] = value[4 * s:4 * s + 4]
 
-    def left_sum(step, part, core, rows, zs, own_half, finish, after_core, after_xy):
+    def left_sum(step, part, rows, zs, own_half, finish, after_send):
         sems = p_sem.at[step]
-        send(part.at[1 - c], core, pair(sems, 0), core_peer)
-        sent.append((core, sems.at[0, 0]))
-        after_core()
-        own_half()
-        took(core, sems.at[0, 1])
-        for dx, dy in PLANE:
-            px, py = (x + dx) % NX, (y + dy) % NY
-            slot = px * NY + py
-            part[c, slot] = part[c, slot] + core[slot]
-            send(part.at[c, slot], rows.at[dx * NY + dy - 1], pair(sems, 1), place(px, z, py, c))
-        sent.append((rows, sems.at[1, 0]))
-        after_xy()
-        part[c, me] = part[c, me] + core[me]
-        took(rows, sems.at[1, 1])
+        for core in (1, 0):
+            half = (c + core) % 2
+            for dx, dy in PLANE:
+                if (dx, dy, core) != (0, 0, 0):
+                    px, py = (x + dx) % NX, (y + dy) % NY
+                    slot = 16 * core + 4 * dx + dy - 1
+                    send(part.at[half, px * NY + py], rows.at[slot], pair(sems, 0), place(px, z, py, half))
+            if core == 1:
+                own_half()
+        sent.append((rows, sems.at[0, 0]))
+        after_send()
+        took(rows, sems.at[0, 1])
         zs[z] = part[c, me] + jnp.sum(rows[...], axis=0)
         for k in RING16:
-            send(zs.at[z], zs.at[z], pair(sems, 2), at_z(k))
-        sent.append((zs.at[pl.ds(0, 15)], sems.at[2, 0]))
-        took(zs.at[pl.ds(0, 15)], sems.at[2, 1])
+            send(zs.at[z], zs.at[z], pair(sems, 1), at_z(k))
+        sent.append((zs.at[pl.ds(0, 15)], sems.at[1, 0]))
+        took(zs.at[pl.ds(0, 15)], sems.at[1, 1])
         pf[step, c, me] = finish(jnp.sum(zs[...], axis=0))
-        for dx, dy in PLANE:
-            device = place((x + dx) % NX, z, (y + dy) % NY, c)
-            send(pf.at[step, c, me], pf.at[step, c, me], pair(sems, 3), device)
-        sent.append((pf.at[step, c, pl.ds(0, 15)], sems.at[3, 0]))
-        took(pf.at[step, c, pl.ds(0, 15)], sems.at[3, 1])
-        send(pf.at[step, c], pf.at[step, c], pair(sems, 4), core_peer)
-        sent.append((pf.at[step, c], sems.at[4, 0]))
+        mine = pf.at[step, c, me]
+        for core in (1, 0):
+            for dx, dy in PLANE:
+                if (dx, dy, core) != (0, 0, 0):
+                    device = place((x + dx) % NX, z, (y + dy) % NY, (c + core) % 2)
+                    send(mine, mine, (sems.at[2 + core, 0], sems.at[2 + core, 1]), device)
+        sent.append((pf.at[step, c, pl.ds(0, 15)], sems.at[2, 0]))
+        sent.append((pf.at[step, c], sems.at[3, 0]))
+        took(pf.at[step, c, pl.ds(0, 15)], sems.at[2, 1])
 
     def half_of(step, h):
         return jnp.concatenate([pf[step, h, s] for s in range(16)], axis=0)
@@ -182,7 +182,7 @@
             cols = slice(BAND * jx, BAND * (jx + 1))
             terms = dot(weighted, g[half_rows(c), cols], NN) + dot(plain, r[half_rows(c), cols], NN)
             qs[step, jx] = fold(terms).reshape(4, 16, BAND)
-        took(pf.at[step, 1 - c], p_sem.at[step, 4, 1])
+        took(pf.at[step, 1 - c], p_sem.at[step, 3, 1])
         other = half_of(step, 1 - c)
         plain, weighted = tall(other), tall(weight * other)
         for dx in RING4:
@@ -246,10 +246,9 @@
     count_x[0] = jnp.full((1, 128), tokens, F32)
     pl.semaphore_wait(barrier, PARTNERS)
 
-    def count_to_x():
-        for k in (2, 1, 3):
-            send(count_x.at[0], count_x.at[k], pair(count_sem, 0), place((x + k) % NX, z, y, c))
-        sent.append((count_x.at[pl.ds(1, 3)], count_sem.at[0, 0]))
+    for k in (2, 1, 3):
+        send(count_x.at[0], count_x.at[k], pair(count_sem, 0), place((x + k) % NX, z, y, c))
+    sent.append((count_x.at[pl.ds(1, 3)], count_sem.at[0, 0]))
 
     def count_to_z():
         took(count_x.at[pl.ds(1, 3)], count_sem.at[0, 1])
@@ -264,7 +263,7 @@
         return (total[:4] * (REPLICAS / all_tokens) + total[4:]) * (1.0 / REPLICAS)
 
     nothing = lambda: None
-    left_sum(0, part1, core1, rows1, zs1, nothing, finish_first, count_to_x, count_to_z)
+    left_sum(0, part1, rows1, zs1, nothing, finish_first, count_to_z)
     weight = REPLICAS * tokens / jnp.sum(count_z[...], axis=0)[:, :1]
 
     kept = []
@@ -291,7 +290,7 @@
     def own_half():
         put_part(part2, c, p_acc[c] + left_terms(plain, weighted, c, cols), 0)
 
-    left_sum(1, part2, core2, rows2, zs2, own_half, lambda total: total * (1.0 / REPLICAS), nothing, nothing)
+    left_sum(1, part2, rows2, zs2, own_half, lambda total: total * (1.0 / REPLICAS), nothing)
 
     def last_left(lower_inverse, p_sum):
         p_basis = lax.dot_general(lower_inverse, p_sum, NN, precision=HIGHEST, preferred_element_type=F32)
@@ -303,24 +302,18 @@
     right_sum(1, weight, last_left)
     p_left = kept.pop()
     inverse_left = kept.pop()
-    stores = []
     for dx, cols, band in bands(1, inverse_left):
         q_final[:, cols] = band
         approx = dot(p_left, right_factor(band), NN)
         matrix = weight * g[:, cols].astype(F32) + r[:, cols].astype(F32)
-        out[:, cols] = (matrix - approx).astype(BF16)
-        store = pltpu.make_async_copy(out.at[:, cols], new_residual.at[0, :, cols], store_sem.at[dx])
-        store.start()
-        stores.append(store)
-    for store in stores:
-        store.wait()
+        new_residual[0, :, cols] = (matrix - approx).astype(BF16)
     for ref, sem in sent:
         took(ref, sem)
 
 
 def local(grad, residual, counts, q_start):
     vmem = pl.BlockSpec(memory_space=pltpu.VMEM)
-    anywhere = pl.BlockSpec(memory_space=pl.ANY)
+    hbm = pl.BlockSpec(memory_space=pltpu.HBM)
     dma = pltpu.SemaphoreType.DMA
     return pl.pallas_call(
         kernel,
@@ -328,28 +321,24 @@
             jax.ShapeDtypeStruct((1, ROWS, WIDTH), BF16),
             jax.ShapeDtypeStruct((RANK, WIDTH), F32),
         ),
-        in_specs=[pl.BlockSpec(memory_space=pltpu.SMEM), anywhere, anywhere, anywhere],
-        out_specs=(anywhere, vmem),
+        in_specs=[pl.BlockSpec(memory_space=pltpu.SMEM), hbm, hbm, hbm],
+        out_specs=(vmem, vmem),
         scratch_shapes=[
             pltpu.VMEM((RANK, WIDTH), F32),
             pltpu.VMEM((ROWS, WIDTH), BF16),
             pltpu.VMEM((ROWS, WIDTH), BF16),
-            pltpu.VMEM((ROWS, WIDTH), BF16),
             dma((3,)),
-            dma((4,)),
             pltpu.VMEM((4, 1, 128), F32),
             pltpu.VMEM((16, 1, 128), F32),
             dma((2, 2)),
             pltpu.VMEM((2, 16, 8, HALF), F32),
-            pltpu.VMEM((16, 8, HALF), F32),
-            pltpu.VMEM((15, 8, HALF), F32),
+            pltpu.VMEM((31, 8, HALF), F32),
             pltpu.VMEM((16, 8, HALF), F32),
             pltpu.VMEM((2, 16, 4, HALF), F32),
-            pltpu.VMEM((16, 4, HALF), F32),
-            pltpu.VMEM((15, 4, HALF), F32),
+            pltpu.VMEM((31, 4, HALF), F32),
             pltpu.VMEM((16, 4, HALF), F32),
             pltpu.VMEM((2, 2, 16, 4, HALF), F32),
-            dma((2, 5, 2)),
+            dma((2, 4, 2)),
             pltpu.VMEM((2, 4, 4, 16, BAND), F32),
             pltpu.VMEM((2, 15, 16, BAND), F32),
             pltpu.VMEM((2, 4, 16, BAND), F32),
@@ -360,10 +349,10 @@
             pltpu.VMEM((2, RANK, HALF), F32),
         ],
         compiler_params=pltpu.CompilerParams(
-            collective_id=0, has_side_effects=True, vmem_limit_bytes=60 * 1024 * 1024
+            collective_id=0, has_side_effects=True, vmem_limit_bytes=32 * 1024 * 1024
         ),
         name="power_step",
-    )(counts, q_start, grad, residual)
+    )(counts, *(pltpu.with_memory_space_constraint(a, pltpu.HBM) for a in (q_start, grad, residual)))
 
 
 def solution(mesh):

time: 107 us -> 101 us (0.944)
  Pallas kernels: 102 us -> 97.3 us
  local copies, waits for them, and re-layouts: 3.42 us -> 1.85 us
    pallas_call x1, Pallas kernels: 102 us -> 97.3 us  [local(): pl.pallas_call(kernel, out_shape=(jax.ShapeDtypeStruct((1, ROWS, WIDTH),...]
    unnamed x4 -> x2, local copies, waits for them, and re-layouts: 3.42 us -> 1.85 us
where the time goes in v3:
time: 101 us; the launch traced here: 100 us
  Pallas kernels  97.3 us (96%)
  local copies, waits for them, and re-layouts  1.85 us (2%)
  between operations  1.28 us (1%)
    pallas_call x1, Pallas kernels, local(): pl.pallas_call(kernel, out_shape=(jax.ShapeDtypeStruct((1, ROWS, WIDTH),...  97.3 us

profile of v3, /device:TPU:1, one launch (start us, length us, event | category | flops | bytes accessed | tf_op | source)
XLA Modules:
  0.0 100.4 jit_solution(9119214338811334429)
XLA Ops:
  1.3 97.3 %power_step.1 = (bf16[1,768,1024]{2,1,0:T(8,128)(2,1)S(1)}, f32[64,1024]{1,0:T(8,128)S(1)}) custom-call(s32[1]{0:T(128)S(6)} %copy.8.counts, f32[64,1024]{1,0:T(8,128)} %q_start.1, bf16[1,768,1024]{2,1,0:T(8,128)(2,1)} %grad.1, bf16[1,768,1024]{2,1,0:T(8,128)(2,1)} %residual.1), custom_call_target="tpu_custom_call" | custom-call | tf_op jit(solution)/shard_map/power_step/pallas_call | solution.py:318
  98.5 1.1 %copy.9 = bf16[1,768,1024]{2,1,0:T(8,128)(2,1)} copy(bf16[1,768,1024]{2,1,0:T(8,128)(2,1)S(1)} %get-tuple-element.4) | data formatting | bytes 3145728
  99.7 0.7 copy.10

commit v4 on v3

--- a/solution.py
+++ b/solution.py
@@ -176,26 +176,19 @@
 
     def right_sum(step, weight, use):
         sems = q_sem.at[step]
-        own = half_of(step, c)
-        plain, weighted = tall(own), tall(weight * own)
-        for jx in range(NX):
-            cols = slice(BAND * jx, BAND * (jx + 1))
-            terms = dot(weighted, g[half_rows(c), cols], NN) + dot(plain, r[half_rows(c), cols], NN)
-            qs[step, jx] = fold(terms).reshape(4, 16, BAND)
         took(pf.at[step, 1 - c], p_sem.at[step, 3, 1])
-        other = half_of(step, 1 - c)
-        plain, weighted = tall(other), tall(weight * other)
+        p_sum = jnp.concatenate([half_of(step, 0), half_of(step, 1)], axis=1)
+        plain, weighted = tall(p_sum), tall(weight * p_sum)
         for dx in RING4:
             px = (x + dx) % NX
-            rows, cols = half_rows(1 - c), band_cols(px)
-            terms = dot(weighted, g[rows, cols], NN) + dot(plain, r[rows, cols], NN)
-            qs[step, px] = qs[step, px] + fold(terms).reshape(4, 16, BAND)
+            cols = band_cols(px)
+            terms = dot(weighted, g[:, cols], NN) + dot(plain, r[:, cols], NN)
+            qs[step, px] = fold(terms).reshape(4, 16, BAND)
             for o in RING4:
                 if (dx, o) != (0, 0):
                     pz = window_z(o)
                     send(qs.at[step, px, pz % 4], near.at[step, dx * 4 + o - 1], pair(sems, 0), place(px, pz, y, c))
         sent.append((near.at[step], sems.at[0, 0]))
-        p_sum = jnp.concatenate([half_of(step, 0), half_of(step, 1)], axis=1)
         diagonal = (
             lax.broadcasted_iota(jnp.int32, (RANK, 2 * RANK), 0)
             == lax.broadcasted_iota(jnp.int32, (RANK, 2 * RANK), 1)
@@ -270,25 +263,25 @@
     right_sum(0, weight, lambda lower_inverse, p_sum: kept.append(left_factor(lower_inverse)))
     inverse_left = kept.pop()
 
-    def left_terms(plain, weighted, h, cols):
-        rows = half_rows(h)
+    def left_terms(plain, weighted, rows, cols):
         return fold(dot(weighted, g[rows, cols], NT) + dot(plain, r[rows, cols], NT))
 
     for dx, cols, band in bands(0, inverse_left):
         plain, weighted = tall(band), tall(weight * band)
-        terms = left_terms(plain, weighted, 1 - c, cols)
         if dx == 0:
-            p_acc[1 - c] = terms
+            p_acc[...] = left_terms(plain, weighted, slice(None), cols)
         elif dx != 2:
-            p_acc[1 - c] = p_acc[1 - c] + terms
-        else:
-            put_part(part2, 1 - c, p_acc[1 - c] + terms, 0)
-            break
-        terms = left_terms(plain, weighted, c, cols)
-        p_acc[c] = terms if dx == 0 else p_acc[c] + terms
+            p_acc[...] = p_acc[...] + left_terms(plain, weighted, slice(None), cols)
+    last = cols
+
+    def put_half(h):
+        terms = left_terms(plain, weighted, half_rows(h), last)
+        put_part(part2, h, p_acc[:, half_rows(h)] + terms, 0)
+
+    put_half(1 - c)
 
     def own_half():
-        put_part(part2, c, p_acc[c] + left_terms(plain, weighted, c, cols), 0)
+        put_half(c)
 
     left_sum(1, part2, rows2, zs2, own_half, lambda total: total * (1.0 / REPLICAS), nothing)
 
@@ -298,6 +291,8 @@
         low = p_basis - high
         kept.append(left_factor(lower_inverse))
         kept.append(jnp.concatenate([high, high, low, low], axis=0).T.astype(BF16))
+        while len(sent) > 4:
+            took(*sent.pop(0))
 
     right_sum(1, weight, last_left)
     p_left = kept.pop()
@@ -311,11 +306,23 @@
         took(ref, sem)
 
 
+def store(residual_in, q_in, residual_out, q_out, sems):
+    copies = [
+        pltpu.make_async_copy(residual_in, residual_out, sems.at[0]),
+        pltpu.make_async_copy(q_in, q_out, sems.at[1]),
+    ]
+    for copy in copies:
+        copy.start()
+    for copy in copies:
+        copy.wait()
+
+
 def local(grad, residual, counts, q_start):
     vmem = pl.BlockSpec(memory_space=pltpu.VMEM)
     hbm = pl.BlockSpec(memory_space=pltpu.HBM)
     dma = pltpu.SemaphoreType.DMA
-    return pl.pallas_call(
+    operands = [pltpu.with_memory_space_constraint(a, pltpu.HBM) for a in (q_start, grad, residual)]
+    results = pl.pallas_call(
         kernel,
         out_shape=(
             jax.ShapeDtypeStruct((1, ROWS, WIDTH), BF16),
@@ -346,13 +353,24 @@
             dma((2, 3, 2)),
             dma((2, 4)),
             pltpu.VMEM((RANK, 2 * RANK), F32),
-            pltpu.VMEM((2, RANK, HALF), F32),
+            pltpu.VMEM((RANK, ROWS), F32),
         ],
         compiler_params=pltpu.CompilerParams(
             collective_id=0, has_side_effects=True, vmem_limit_bytes=32 * 1024 * 1024
         ),
         name="power_step",
-    )(counts, *(pltpu.with_memory_space_constraint(a, pltpu.HBM) for a in (q_start, grad, residual)))
+    )(counts, *operands)
+    return pl.pallas_call(
+        store,
+        out_shape=(
+            jax.ShapeDtypeStruct((1, ROWS, WIDTH), BF16),
+            jax.ShapeDtypeStruct((RANK, WIDTH), F32),
+        ),
+        in_specs=[vmem, vmem],
+        out_specs=(hbm, hbm),
+        scratch_shapes=[dma((2,))],
+        name="store",
+    )(*(pltpu.with_memory_space_constraint(a, pltpu.VMEM) for a in results))
 
 
 def solution(mesh):

time: 101 us -> 101 us (level)
  Pallas kernels: 97.3 us -> 99.2 us
  local copies, waits for them, and re-layouts: 1.85 us -> 0 us
    unnamed x2 -> x0, local copies, waits for them, and re-layouts: 1.85 us -> none
    pallas_call x0 -> x1, Pallas kernels: none -> 1.24 us  [local(): pl.pallas_call(store, out_shape=(jax.ShapeDtypeStruct((1, ROWS, WIDTH), B...]
where the time goes in v4:
time: 101 us; the launch traced here: 100 us
  Pallas kernels  99.2 us (98%)
  between operations  1.28 us (1%)
    pallas_call x1, Pallas kernels, local(): pl.pallas_call(kernel, out_shape=(jax.ShapeDtypeStruct((1, ROWS, WIDTH),...  98 us

profile of v4, /device:TPU:1, one launch (start us, length us, event | category | flops | bytes accessed | tf_op | source)
XLA Modules:
  0.0 100.5 jit_solution(16239734774984213519)
XLA Ops:
  1.3 98.0 %power_step.1 = (bf16[1,768,1024]{2,1,0:T(8,128)(2,1)S(1)}, f32[64,1024]{1,0:T(8,128)S(1)}) custom-call(s32[1]{0:T(128)S(6)} %copy.6.counts, f32[64,1024]{1,0:T(8,128)} %q_start.1, bf16[1,768,1024]{2,1,0:T(8,128)(2,1)} %grad.1, bf16[1,768,1024]{2,1,0:T(8,128)(2,1)} %residual.1), custom_call_target="tpu_custom_call" | custom-call | tf_op jit(solution)/shard_map/power_step/pallas_call | solution.py:325
  99.2 1.2 %store.1 = (bf16[1,768,1024]{2,1,0:T(8,128)(2,1)}, f32[64,1024]{1,0:T(8,128)}) custom-call(bf16[1,768,1024]{2,1,0:T(8,128)(2,1)S(1)} %get-tuple-element.4.residual_in, f32[64,1024]{1,0:T(8,128)S(1)} %get-tuple-element.5.q_in), custom_call_target="tpu_custom_call" | custom-call | tf_op jit(solution)/shard_map/store/pallas_call | solution.py:363

commit v5 on v4

--- a/solution.py
+++ b/solution.py
@@ -14,7 +14,7 @@
 NX, NY, NZ = 4, 4, 16
 NN = (((1,), (0,)), ((), ()))
 NT = (((1,), (1,)), ((), ()))
-PARTNERS = 58
+PARTNERS = 51
 RING4 = (2, 1, 3, 0)
 RING16 = (8, 7, 9, 6, 10, 5, 11, 4, 12, 3, 13, 2, 14, 1, 15)
 PLANE = tuple((i, j) for i in RING4 for j in RING4)
@@ -56,7 +56,7 @@
            q0, g, r, load_sem,
            count_x, count_z, count_sem,
            part1, rows1, zs1, part2, rows2, zs2, pf, p_sem,
-           qs, near, far, qf, q_sem, spread_sem, elim, p_acc):
+           qs, near, far, qf, q_sem, spread_sem, elim, p_acc, relay):
     dp = lax.axis_index("dp")
     tensor = lax.axis_index("tensor")
     x, z, y, c = dp // NZ, dp % NZ, tensor // 2, tensor % 2
@@ -84,7 +84,7 @@
     def announce(device):
         pl.semaphore_signal(barrier, inc=1, device_id=device, device_id_type=MESH)
 
-    for k in RING16:
+    for k in (4, 12, 3, 13, 2, 14, 1, 15):
         announce(at_z(k))
     for dx, dy in PLANE:
         for core in (1, 0):
@@ -238,6 +238,8 @@
         put_part(part1, h, fold(dot(first, r[rows], NT)), 4)
     count_x[0] = jnp.full((1, 128), tokens, F32)
     pl.semaphore_wait(barrier, PARTNERS)
+    for k in (4, 12):
+        pl.semaphore_signal(relay, inc=1, device_id=at_z(k), device_id_type=MESH)
 
     for k in (2, 1, 3):
         send(count_x.at[0], count_x.at[k], pair(count_sem, 0), place((x + k) % NX, z, y, c))
@@ -245,6 +247,7 @@
 
     def count_to_z():
         took(count_x.at[pl.ds(1, 3)], count_sem.at[0, 1])
+        pl.semaphore_wait(relay, 2)
         count_z[z] = jnp.sum(count_x[...], axis=0)
         for k in RING16:
             send(count_z.at[z], count_z.at[z], pair(count_sem, 1), at_z(k))
@@ -354,6 +357,7 @@
             dma((2, 4)),
             pltpu.VMEM((RANK, 2 * RANK), F32),
             pltpu.VMEM((RANK, ROWS), F32),
+            pltpu.SemaphoreType.REGULAR,
         ],
         compiler_params=pltpu.CompilerParams(
             collective_id=0, has_side_effects=True, vmem_limit_bytes=32 * 1024 * 1024

time: 101 us -> 100 us (0.990)
  Pallas kernels: 99.2 us -> 97.9 us
    pallas_call x1, Pallas kernels: 98 us -> 96.6 us  [local(): pl.pallas_call(kernel, out_shape=(jax.ShapeDtypeStruct((1, ROWS, WIDTH),...]
where the time goes in v5:
time: 100 us; the launch traced here: 99.2 us
  Pallas kernels  97.9 us (98%)
  between operations  1.28 us (1%)
    pallas_call x1, Pallas kernels, local(): pl.pallas_call(kernel, out_shape=(jax.ShapeDtypeStruct((1, ROWS, WIDTH),...  96.6 us

profile of v5, /device:TPU:1, one launch (start us, length us, event | category | flops | bytes accessed | tf_op | source)
XLA Modules:
  0.0 99.2 jit_solution(17560774090269871507)
XLA Ops:
  1.3 96.6 %power_step.1 = (bf16[1,768,1024]{2,1,0:T(8,128)(2,1)S(1)}, f32[64,1024]{1,0:T(8,128)S(1)}) custom-call(s32[1]{0:T(128)S(6)} %copy.6.counts, f32[64,1024]{1,0:T(8,128)} %q_start.1, bf16[1,768,1024]{2,1,0:T(8,128)(2,1)} %grad.1, bf16[1,768,1024]{2,1,0:T(8,128)(2,1)} %residual.1), custom_call_target="tpu_custom_call" | custom-call | tf_op jit(solution)/shard_map/power_step/pallas_call | solution.py:328
  97.9 1.2 %store.1 = (bf16[1,768,1024]{2,1,0:T(8,128)(2,1)}, f32[64,1024]{1,0:T(8,128)}) custom-call(bf16[1,768,1024]{2,1,0:T(8,128)(2,1)S(1)} %get-tuple-element.4.residual_in, f32[64,1024]{1,0:T(8,128)S(1)} %get-tuple-element.5.q_in), custom_call_target="tpu_custom_call" | custom-call | tf_op jit(solution)/shard_map/store/pallas_call | solution.py:367
